TPU v7x, 32 devices: a whole 2x2x4 slice. The times are simulated.
32 devices in a mesh: parts: 2 (over x), loop: 16 (over z, y, core).
Axes of the slice: x: 2, y: 2, z: 4, core: 2. Of those that a mesh axis runs over, the one named last changes fastest.
Arguments:
- leaf_rows: bfloat16 [128, 8192], P(('parts', 'loop')), parts along dimension 0, may hold values from -6 to 6
- norm_gain: float32 [8192], replicated, may hold values from 0.5 to 1.5
- gate_weight: bfloat16 [16, 1024, 13312], P('loop'), may hold values from -0.0625 to 0.0625
- up_weight: bfloat16 [16, 1024, 13312], P('loop'), may hold values from -0.0625 to 0.0625
- down_weight: bfloat16 [16, 13312, 1024], P('loop'), may hold values from -0.0390625 to 0.0390625
Outputs:
- leaf_output: bfloat16 [128, 8192], P(('parts', 'loop')), parts along dimension 0
There are 2 independent parts, one for each index of `parts`. A program takes and returns all parts, laid end to end along the dimension named above; an argument that names none is the same for every part. Nothing has to cross between parts.
All inputs are finite; a program needn't handle non-finite values.
Results may differ from a plain program's by a relative error of at most 0.0048.
Values may be sent and summed in bfloat16 or wider, within the bound.
A program may use at most 192 MiB of HBM per device.

v0:
```python
import jax
import jax.numpy as jnp
from jax import lax
from jax.sharding import PartitionSpec as P

FEAT_GROUPS = 8


epsilon = 1e-05


def swapped(value, axis, apart):
    mask = 2**apart
    pairs = [(source, source ^ mask) for source in range(lax.axis_size(axis))]
    return lax.ppermute(value, axis, pairs)


def normalize(leaf_rows, norm_gain):
    values = leaf_rows.astype(jnp.float32)
    inverse = lax.rsqrt(jnp.mean(values * values, axis=1, keepdims=True) + epsilon)
    return (values * inverse * norm_gain).astype(jnp.bfloat16)


def per_device(leaf_rows, norm_gain, gate_weight, up_weight, down_weight):
    gate_block = gate_weight[0]
    up_block = up_weight[0]
    down_block = down_weight[0]
    width = gate_block.shape[0]
    hid_width = gate_block.shape[1]
    groups = FEAT_GROUPS
    own_rows = leaf_rows.shape[0]
    place = lax.axis_index("loop")
    count = lax.axis_size("loop")
    nbits = count.bit_length() - 1
    feat = place % groups
    normed = normalize(leaf_rows, norm_gain)
    row_slice = lax.dynamic_slice_in_dim(
        lax.all_gather(normed, "loop", axis=0, tiled=True), feat * width, width, 1
    )
    gate_sum = jnp.dot(row_slice, gate_block, preferred_element_type=jnp.float32)
    up_sum = jnp.dot(row_slice, up_block, preferred_element_type=jnp.float32)
    both = jnp.concatenate([gate_sum, up_sum], axis=1)
    current = both
    for bit in (2, 1, 0):
        half = current.shape[0] // 2
        mine = place // (1 << bit) % 2
        keep = lax.dynamic_slice_in_dim(current, mine * half, half, 0)
        other = lax.dynamic_slice_in_dim(current, (1 - mine) * half, half, 0)
        current = keep + swapped(other, "loop", bit)
    hidden = (jax.nn.silu(current[:, :hid_width]) * current[:, hid_width:]).astype(jnp.bfloat16)
    for bit in (0, 1, 2):
        mine = place // (1 << bit) % 2
        received = swapped(hidden, "loop", bit)
        hidden = jnp.where(
            mine == 0,
            jnp.concatenate([hidden, received], 0),
            jnp.concatenate([received, hidden], 0),
        )
    current = jnp.dot(hidden, down_block, preferred_element_type=jnp.float32)
    for bit in range(nbits - 1, 2, -1):
        half = current.shape[0] // 2
        mine = place // (1 << bit) % 2
        keep = lax.dynamic_slice_in_dim(current, mine * half, half, 0)
        other = lax.dynamic_slice_in_dim(current, (1 - mine) * half, half, 0)
        current = keep + swapped(other, "loop", bit)
    pieces = current.reshape(2, 2, 2, own_rows, width)
    for bit in (0, 1, 2):
        where_axis = 2 - bit
        mine = place // (1 << bit) % 2
        keep = lax.dynamic_index_in_dim(pieces, mine, where_axis, keepdims=False)
        other = lax.dynamic_index_in_dim(pieces, 1 - mine, where_axis, keepdims=False)
        received = swapped(other, "loop", bit)
        pieces = jnp.where(
            mine == 0,
            jnp.stack([keep, received], where_axis),
            jnp.stack([received, keep], where_axis),
        )
    branch = jnp.transpose(pieces.reshape(groups, own_rows, width), (1, 0, 2)).reshape(
        own_rows, groups * width
    )
    return (leaf_rows.astype(jnp.float32) + branch).astype(jnp.bfloat16)


def solution(mesh):
    return jax.shard_map(
        per_device,
        mesh=mesh,
        in_specs=(
            P(("parts", "loop"), None),
            P(),
            P("loop", None, None),
            P("loop", None, None),
            P("loop", None, None),
        ),
        out_specs=P(("parts", "loop"), None),
        check_vma=False,
    )
```

profile of v0, /device:TPU:0, one launch (start us, length us, event | category | flops | bytes accessed | tf_op | source)
XLA Modules:
  0.0 272.3 jit_solution(2113247566268465537)
XLA Ops:
  6.5 0.0 all-gather.3.cloned.1.call-start
  6.5 1.0 fusion.16
  7.6 1.6 fusion.22
  9.1 0.0 all-gather.3.cloned.1.call-update
  9.2 41.0 %all-gather.3.cloned.1.call-done = bf16[16,4,8192]{2,1,0:T(4,128)(2,1)} async-done(((bf16[1,4,8192]{2,1,0:T(4,128)(2,1)}), bf16[16,4,8192]{2,1,0:T(4,128)(2,1)}) %all-gather.3.cloned.1.call-update) | async-done | bytes 1048592 | tf_op jit(solution)/shard_map/all_gather | solution.py:38
  50.2 2.1 reshape.23
  52.3 11.3 %fusion.2 = f32[64,13312]{1,0:T(8,128)S(1)} fusion(bf16[1,1024,13312]{2,1,0:T(8,128)(2,1)} %param.8, bf16[64,8192]{1,0:T(8,128)(2,1)} %reshape.23, s32[]{:T(128)S(6)} %select_n.160), kind=kOutput, calls=%fused_computation.2 | convolution fusion | flops 1744830464 | bytes 30801924 | tf_op jit(solution)/shard_map/dot_general | solution.py:41
  63.6 11.3 %fusion.4 = f32[64,13312]{1,0:T(8,128)S(1)} fusion(bf16[1,1024,13312]{2,1,0:T(8,128)(2,1)} %param.7, bf16[64,8192]{1,0:T(8,128)(2,1)} %reshape.23, s32[]{:T(128)S(6)} %select_n.160), kind=kOutput, calls=%fused_computation.4 | convolution fusion | flops 1744830464 | bytes 30801924 | tf_op jit(solution)/shard_map/dot_general | solution.py:40
  74.9 0.0 copy-start
  74.9 2.2 fusion.6
  77.1 0.7 copy-done
  77.8 0.5 collective-permute-start
  78.3 75.7 %collective-permute-done = f32[32,26624]{1,0:T(8,128)} collective-permute-done((f32[32,26624]{1,0:T(8,128)}, f32[32,26624]{1,0:T(8,128)}, u32[]{:S(2)}, u32[]{:S(2)}) %collective-permute-start) | collective-permute-done | bytes 3407904 | tf_op jit(solution)/shard_map/ppermute | solution.py:15
  154.0 2.8 %fusion.8 = f32[32,26624]{1,0:T(8,128)S(1)} fusion(f32[32,26624]{1,0:T(8,128)} %collective-permute-done, s32[]{:T(128)S(6)} %select_n.161, f32[64,13312]{1,0:T(8,128)} %copy-done, f32[64,13312]{1,0:T(8,128)S(1)} %fusion.2), kind=kLoop, calls=%fused_computation.12 | loop fusion | flops 1703936 | bytes 13631492 | tf_op jit(solution)/shard_map/add | solution.py:49
  156.8 0.0 copy-start.1
  156.8 1.7 copy-done.1
  158.5 0.1 constant_dynamic-slice_fusion.5
  158.6 0.6 collective-permute-start.1
  159.2 38.1 %collective-permute-done.1 = f32[16,26624]{1,0:T(8,128)S(1)} collective-permute-done((f32[16,26624]{1,0:T(8,128)S(1)}, f32[16,26624]{1,0:T(8,128)S(1)}, u32[]{:S(2)}, u32[]{:S(2)}) %collective-permute-start.1) | collective-permute-done | bytes 1703968 | tf_op jit(solution)/shard_map/ppermute | solution.py:15
  197.2 1.6 dynamic-slice_add_fusion
  198.9 0.1 constant_dynamic-slice_fusion.4
  198.9 0.1 collective-permute-start.2
  199.0 2.4 collective-permute-done.2
  201.4 0.1 dynamic-slice_add_fusion.1
  201.5 0.1 fusion.15
  201.6 0.2 collective-permute-start.3
  201.8 1.3 collective-permute-done.3
  203.1 0.1 maximum_select_fusion.3
  203.2 0.6 collective-permute-start.4
  203.8 11.4 %collective-permute-done.4 = bf16[16,13312]{1,0:T(8,128)(2,1)S(1)} collective-permute-done((bf16[16,13312]{1,0:T(8,128)(2,1)S(1)}, bf16[16,13312]{1,0:T(8,128)(2,1)S(1)}, u32[]{:S(2)}, u32[]{:S(2)}) %collective-permute-start.4) | collective-permute-done | bytes 426016 | tf_op jit(solution)/shard_map/ppermute | solution.py:15
  215.1 0.1 maximum_select_fusion.2
  215.3 0.6 collective-permute-start.5
  215.9 0.0 copy-start.2
  215.9 19.6 %collective-permute-done.5 = bf16[32,13312]{1,0:T(8,128)(2,1)S(1)} collective-permute-done((bf16[32,13312]{1,0:T(8,128)(2,1)S(1)}, bf16[32,13312]{1,0:T(8,128)(2,1)S(1)}, u32[]{:S(2)}, u32[]{:S(2)}) %collective-permute-start.5) | collective-permute-done | bytes 852000 | tf_op jit(solution)/shard_map/ppermute | solution.py:15
  235.5 11.3 %fusion = f32[64,1024]{1,0:T(8,128)S(1)} fusion(bf16[1,13312,1024]{2,1,0:T(8,128)(2,1)} %param.9, bf16[32,13312]{1,0:T(8,128)(2,1)S(1)} %collective-permute-done.5, bf16[32,13312]{1,0:T(8,128)(2,1)S(1)} %maximum_select_fusion.2, pred[]{:T(512)S(6)} %eq.24), kind=kOutput, calls=%fused_computation | convolution fusion | flops 1752498176 | bytes 29229056 | tf_op jit(solution)/shard_map/dot_general | solution.py:59
  246.8 1.4 collective-permute-start.6
  248.3 6.1 %collective-permute-done.6 = f32[32,1024]{1,0:T(8,128)S(1)} collective-permute-done((f32[32,1024]{1,0:T(8,128)S(1)}, f32[32,1024]{1,0:T(8,128)S(1)}, u32[]{:S(2)}, u32[]{:S(2)}) %collective-permute-start.6) | collective-permute-done | bytes 131104 | tf_op jit(solution)/shard_map/ppermute | solution.py:15
  254.5 0.1 collective-permute-start.7
  254.5 1.2 collective-permute-done.7
  255.8 0.6 collective-permute-start.8
  256.4 3.7 %collective-permute-done.8 = f32[2,2,4,1024]{3,2,1,0:T(4,128)S(1)} collective-permute-done((f32[2,2,4,1024]{3,2,1,0:T(4,128)S(1)}, f32[2,2,4,1024]{3,2,1,0:T(4,128)S(1)}, u32[]{:S(2)}, u32[]{:S(2)}) %collective-permute-start.8) | collective-permute-done | bytes 65568 | tf_op jit(solution)/shard_map/ppermute | solution.py:15
  260.2 0.1 collective-permute-start.9
  260.3 4.3 %collective-permute-done.9 = f32[2,2,4,1024]{3,2,1,0:T(4,128)S(1)} collective-permute-done((f32[2,2,4,1024]{3,2,1,0:T(4,128)S(1)}, f32[2,2,4,1024]{3,2,1,0:T(4,128)S(1)}, u32[]{:S(2)}, u32[]{:S(2)}) %collective-permute-start.9) | collective-permute-done | bytes 65568 | tf_op jit(solution)/shard_map/ppermute | solution.py:15
  264.6 0.1 copy.10
  264.7 0.1 copy.8
  264.8 0.0 copy-done.2
  264.8 0.7 fusion.19
  (10 shorter events, 0.2 us)
Async XLA Ops:
  6.5 43.7 %all-gather.3.cloned.1.call-start = ((), (), s32[]{:S(2)}) async-start(), calls=%async_computation | async-start | bytes 1114112 | tf_op jit(solution)/shard_map/all_gather | solution.py:38
  74.9 2.8 %copy-start = (f32[64,13312]{1,0:T(8,128)}, f32[64,13312]{1,0:T(8,128)S(1)}, u32[]{:S(2)}) copy-start(f32[64,13312]{1,0:T(8,128)S(1)} %fusion.4) | copy-start | bytes 10223620
  77.8 76.2 %collective-permute-start = (f32[32,26624]{1,0:T(8,128)}, f32[32,26624]{1,0:T(8,128)}, u32[]{:S(2)}, u32[]{:S(2)}) collective-permute-start(f32[32,26624]{1,0:T(8,128)} %fusion.6), channel_id=1, source_target_pairs={{0,4},{1,5},{2,6},{3,7},{4,0},{5,1},{6,2},{7,3},{8,12},{9,13},{10,... | collective-permute-start | bytes 10223624 | tf_op jit(solution)/shard_map/ppermute | solution.py:15
  156.8 1.7 copy-start.1
  158.6 38.6 %collective-permute-start.1 = (f32[16,26624]{1,0:T(8,128)S(1)}, f32[16,26624]{1,0:T(8,128)S(1)}, u32[]{:S(2)}, u32[]{:S(2)}) collective-permute-start(f32[16,26624]{1,0:T(8,128)S(1)} %constant_dynamic-slice_fusion.5), channel_id=1, source_target_pairs={{0,2},{1,3},{2,0},{3,1},{4,6},{5,7},{6,4},{7,5},{8,10},{9,11},{10,... | collective-permute-start | bytes 5111816 | tf_op jit(solution)/shard_map/ppermute | solution.py:15
  198.9 2.4 collective-permute-start.2
  201.6 1.5 collective-permute-start.3
  203.2 11.9 %collective-permute-start.4 = (bf16[16,13312]{1,0:T(8,128)(2,1)S(1)}, bf16[16,13312]{1,0:T(8,128)(2,1)S(1)}, u32[]{:S(2)}, u32[]{:S(2)}) collective-permute-start(bf16[16,13312]{1,0:T(8,128)(2,1)S(1)} %maximum_select_fusion.3), channel_id=1, source_target_pairs={{0,2},{1,3},{2,0},{3,1},{4,6},{5,7},{6,4},{7,5},{8,10},{9,11},{10,... | collective-permute-start | bytes 1277960 | tf_op jit(solution)/shard_map/ppermute | solution.py:15
  215.3 20.2 %collective-permute-start.5 = (bf16[32,13312]{1,0:T(8,128)(2,1)S(1)}, bf16[32,13312]{1,0:T(8,128)(2,1)S(1)}, u32[]{:S(2)}, u32[]{:S(2)}) collective-permute-start(bf16[32,13312]{1,0:T(8,128)(2,1)S(1)} %maximum_select_fusion.2), channel_id=1, source_target_pairs={{0,4},{1,5},{2,6},{3,7},{4,0},{5,1},{6,2},{7,3},{8,12},{9,13},{10,... | collective-permute-start | bytes 2555912 | tf_op jit(solution)/shard_map/ppermute | solution.py:15
  215.9 48.9 %copy-start.2 = (bf16[4,8192]{1,0:T(4,128)(2,1)S(1)}, bf16[4,8192]{1,0:T(4,128)(2,1)}, u32[]{:S(2)}) copy-start(bf16[4,8192]{1,0:T(4,128)(2,1)} %param.5) | copy-start | bytes 196612
  246.8 7.5 %collective-permute-start.6 = (f32[32,1024]{1,0:T(8,128)S(1)}, f32[32,1024]{1,0:T(8,128)S(1)}, u32[]{:S(2)}, u32[]{:S(2)}) collective-permute-start(f32[32,1024]{1,0:T(8,128)S(1)} %constant_dynamic-slice_fusion.3), channel_id=1, source_target_pairs={{0,8},{1,9},{2,10},{3,11},{4,12},{5,13},{6,14},{7,15},{8,0},{9,1},... | collective-permute-start | bytes 393224 | tf_op jit(solution)/shard_map/ppermute | solution.py:15
  254.5 1.3 collective-permute-start.7
  255.8 4.3 %collective-permute-start.8 = (f32[2,2,4,1024]{3,2,1,0:T(4,128)S(1)}, f32[2,2,4,1024]{3,2,1,0:T(4,128)S(1)}, u32[]{:S(2)}, u32[]{:S(2)}) collective-permute-start(f32[2,2,4,1024]{3,2,1,0:T(4,128)S(1)} %get-tuple-element.8), channel_id=1, source_target_pairs={{0,2},{1,3},{2,0},{3,1},{4,6},{5,7},{6,4},{7,5},{8,10},{9,11},{10,... | collective-permute-start | bytes 196616 | tf_op jit(solution)/shard_map/ppermute | solution.py:15
  260.2 4.3 %collective-permute-start.9 = (f32[2,2,4,1024]{3,2,1,0:T(4,128)S(1)}, f32[2,2,4,1024]{3,2,1,0:T(4,128)S(1)}, u32[]{:S(2)}, u32[]{:S(2)}) collective-permute-start(f32[2,2,4,1024]{3,2,1,0:T(4,128)S(1)} %get-tuple-element.6), channel_id=1, source_target_pairs={{0,4},{1,5},{2,6},{3,7},{4,0},{5,1},{6,2},{7,3},{8,12},{9,13},{10,... | collective-permute-start | bytes 196616 | tf_op jit(solution)/shard_map/ppermute | solution.py:15
Sparse Core Ops, SparseCore 0:
  9.5 40.6 all-gather.2
where the time goes:
time: 273 us; the launch traced here: 272 us
  waiting for transfers between devices  205 us (75%)
  matrix products  33.9 us (12%)
  between operations  13.7 us (5%)
  other arithmetic  10.4 us (4%)
  local copies, waits for them, and re-layouts  4.98 us (2%)
  starting transfers between devices  4.69 us (2%)
    ppermute x10, waiting for transfers between devices, swapped(): return lax.ppermute(value, axis, pairs)  164 us
    all_gather x1, waiting for transfers between devices, per_device(): lax.all_gather(normed, 'loop', axis=0, tiled=True)  41 us
    dot_general x1, matrix products, per_device(): current = jnp.dot(hidden, down_block, preferred_element_type=jnp.float32)  11.3 us
    dot_general x1, matrix products, per_device(): jnp.dot(row_slice, gate_block, preferred_element_type=jnp.float32)  11.3 us
    dot_general x1, matrix products, per_device(): up_sum = jnp.dot(row_slice, up_block, preferred_element_type=jnp.float32)  11.3 us
  transfers between devices with their start and end apart: 11, of which 11 were waited for; matrix products, arithmetic and copies ran while one was open for 0% of the time, Pallas kernels for 0%

commit v1 on v0

--- a/solution.py
+++ b/solution.py
@@ -1,12 +1,338 @@
+import functools
+
 import jax
 import jax.numpy as jnp
 from jax import lax
+from jax.experimental import pallas as pl
+from jax.experimental.pallas import tpu as pltpu
 from jax.sharding import PartitionSpec as P
 
 FEAT_GROUPS = 8
-
+CHUNK = 512
+SKEWS = (0, 1, 3, 5, 7, 9, 10)
+VMEM_BYTES = 60 * 2**20
+MESH = pl.DeviceIdType.MESH
 
 epsilon = 1e-05
+
+
+def fused_kernel(
+    sizes, leaf_ref, gain_ref, gate_hbm, up_hbm, down_hbm, out_ref,
+    gate_v, up_v, down_v, x_send, x_recv, x_full, keep,
+    s1, r1, s2, r2, s3, r3, hid, y_acc, y_send, y_recv,
+    w_sem, send_sem, recv_sem, xs_sem, xr_sem, ys_sem, yr_sem,
+):
+    parts, count, own, width, half, chunk = sizes
+    n = parts * count
+    nch = half // chunk
+    rows = own * n
+    split = 16 // own
+    w4 = width // split
+    part = lax.axis_index("parts")
+    place = lax.axis_index("loop")
+    me = part * count + place
+    b0 = lax.rem(place, 2)
+    b1 = lax.rem(place // 2, 2)
+    b2 = lax.rem(place // 4, 2)
+    core_peer = place + 1 - 2 * b0
+    h2, h4, h8 = rows // 2, rows // 4, rows // 8
+
+    def device(index):
+        return {"parts": index // count, "loop": lax.rem(index, count)}
+
+    def bits(j):
+        even = 1 - lax.rem(j, 2)
+        odd = 1 - even
+        first_bit = even * b1 + odd * b2
+        second_bit = even * b2 + odd * b1
+        first_peer = place + (even * 2 + odd * 4) * (1 - 2 * first_bit)
+        second_peer = place + (even * 4 + odd * 2) * (1 - 2 * second_bit)
+        return first_bit, second_bit, first_peer, second_peer
+
+    def load_gate(j):
+        cols = pl.ds(pl.multiple_of(part * half + j * chunk, 128), chunk)
+        return (
+            pltpu.make_async_copy(gate_hbm.at[0, :, cols], gate_v.at[j], w_sem.at[0, j]),
+            pltpu.make_async_copy(up_hbm.at[0, :, cols], up_v.at[j], w_sem.at[1, j]),
+        )
+
+    def load_down(j):
+        at = pl.ds(pl.multiple_of(part * half + j * chunk, 16), chunk)
+        return pltpu.make_async_copy(down_hbm.at[0, at, :], down_v.at[j], w_sem.at[2, j])
+
+    @pl.loop(0, nch)
+    def _(j):
+        for copy in load_gate(j):
+            copy.start()
+
+    @pl.loop(0, nch)
+    def _(j):
+        load_down(j).start()
+
+    barrier = pltpu.get_barrier_semaphore()
+
+    @pl.loop(1, n)
+    def _(k):
+        pl.semaphore_signal(
+            barrier, inc=1, device_id=device(lax.rem(me + k, n)), device_id_type=MESH
+        )
+
+    values = leaf_ref[...].astype(jnp.float32)
+    inverse = lax.rsqrt(jnp.mean(values * values, axis=1, keepdims=True) + epsilon)
+    normed = values * inverse * gain_ref[...]
+    for f in range(FEAT_GROUPS):
+        piece = jnp.concatenate(
+            [normed[:, f * width + c * w4 : f * width + (c + 1) * w4] for c in range(split)], axis=0
+        )
+        x_send[f] = piece.astype(jnp.bfloat16)
+    y_acc[...] = jnp.zeros_like(y_acc)
+    x_recv[me] = x_send[lax.rem(place, FEAT_GROUPS)]
+
+    pl.semaphore_wait(barrier, n - 1)
+
+    def x_copy(to, source):
+        return pltpu.make_async_remote_copy(
+            src_ref=x_send.at[lax.rem(to, FEAT_GROUPS)],
+            dst_ref=x_recv.at[source],
+            send_sem=xs_sem.at[to],
+            recv_sem=xr_sem.at[source],
+            device_id=device(to),
+            device_id_type=MESH,
+        )
+
+    @pl.loop(1, n)
+    def _(k):
+        x_copy(lax.rem(me + k, n), me).start()
+
+    @pl.loop(1, n)
+    def _(k):
+        other = lax.rem(me + k, n)
+        x_copy(other, other).wait_recv()
+
+    group = 16 // own
+    for t in range(rows // 16):
+        base = lax.rem(t + b0 * (rows // 32), rows // 16) * group
+        held = [x_recv[base + s].astype(jnp.float32) for s in range(group)]
+        for c in range(split):
+            tile = jnp.concatenate([h[c * own : (c + 1) * own] for h in held], axis=0)
+            x_full[pl.ds(t * 16, 16), pl.ds(c * w4, w4)] = tile.astype(jnp.bfloat16)
+
+    def remote(stage, j, src, dst, peer):
+        return pltpu.make_async_remote_copy(
+            src_ref=src,
+            dst_ref=dst,
+            send_sem=send_sem.at[stage, j],
+            recv_sem=recv_sem.at[stage, j],
+            device_id={"parts": part, "loop": peer},
+            device_id_type=MESH,
+        )
+
+    def sixteen(value):
+        return pl.multiple_of(value, 16)
+
+    def copy_of(stage, j):
+        fb, sb, fp, sp = bits(j)
+        if stage == 0:
+            return remote(0, j, s1.at[j], r1.at[j], core_peer)
+        if stage == 1:
+            return remote(1, j, s2.at[j], r2.at[j], fp)
+        if stage == 2:
+            return remote(2, j, s3.at[j], r3.at[j], sp)
+        if stage == 3:
+            at = hid.at[j, pl.ds(sixteen(b0 * h2 + fb * h4 + sb * h8), h8), :]
+            return remote(3, j, at, at, sp)
+        if stage == 4:
+            at = hid.at[j, pl.ds(sixteen(b0 * h2 + fb * h4), h4), :]
+            return remote(4, j, at, at, fp)
+        at = hid.at[j, pl.ds(sixteen(b0 * h2), h2), :]
+        return remote(5, j, at, at, core_peer)
+
+    def arrival(stage, j):
+        fb, sb, fp, sp = bits(j)
+        if stage < 3:
+            return copy_of(stage, j)
+        if stage == 3:
+            at = hid.at[j, pl.ds(sixteen(b0 * h2 + fb * h4 + (1 - sb) * h8), h8), :]
+            return remote(3, j, at, at, sp)
+        if stage == 4:
+            at = hid.at[j, pl.ds(sixteen(b0 * h2 + (1 - fb) * h4), h4), :]
+            return remote(4, j, at, at, fp)
+        at = hid.at[j, pl.ds(sixteen((1 - b0) * h2), h2), :]
+        return remote(5, j, at, at, core_peer)
+
+    def project(j):
+        for copy in load_gate(j):
+            copy.wait()
+        for at, weight in ((0, gate_v), (chunk, up_v)):
+            both = jnp.dot(x_full[...], weight[j], preferred_element_type=jnp.float32)
+            keep[j, :, pl.ds(at, chunk)] = both[:h2]
+            s1[j, :, pl.ds(at, chunk)] = both[h2:].astype(jnp.bfloat16)
+        copy_of(0, j).start()
+
+    def partial(j, at, size):
+        at = pl.ds(sixteen(at), size)
+        return keep[j, at, :] + r1[j, at, :].astype(jnp.float32)
+
+    def after_core(j):
+        arrival(0, j).wait_recv()
+        fb, sb, fp, sp = bits(j)
+        s2[j] = partial(j, (1 - fb) * h4, h4).astype(jnp.bfloat16)
+        copy_of(1, j).start()
+
+    def after_first(j):
+        arrival(1, j).wait_recv()
+        fb, sb, fp, sp = bits(j)
+        total = partial(j, fb * h4 + (1 - sb) * h8, h8)
+        total += r2[j, pl.ds(sixteen((1 - sb) * h8), h8), :].astype(jnp.float32)
+        s3[j] = total.astype(jnp.bfloat16)
+        copy_of(2, j).start()
+
+    def after_second(j):
+        fb, sb, fp, sp = bits(j)
+        total = partial(j, fb * h4 + sb * h8, h8)
+        total += r2[j, pl.ds(sixteen(sb * h8), h8), :].astype(jnp.float32)
+        arrival(2, j).wait_recv()
+        total += r3[j].astype(jnp.float32)
+        gate, up = total[:, :chunk], total[:, chunk:]
+        hidden = gate / (1.0 + jnp.exp(-gate)) * up
+        hid[j, pl.ds(sixteen(b0 * h2 + fb * h4 + sb * h8), h8), :] = hidden.astype(jnp.bfloat16)
+        copy_of(3, j).start()
+
+    def gather_first(j):
+        arrival(3, j).wait_recv()
+        copy_of(4, j).start()
+
+    def gather_core(j):
+        arrival(4, j).wait_recv()
+        copy_of(5, j).start()
+
+    def down(j):
+        arrival(5, j).wait_recv()
+        load_down(j).wait()
+        y_acc[...] += jnp.dot(hid[j], down_v[j], preferred_element_type=jnp.float32)
+
+    steps = (project, after_core, after_first, after_second, gather_first, gather_core, down)
+
+    @pl.loop(0, nch + SKEWS[-1])
+    def _(i):
+        for at in (1, 2, 3, 4, 5, 0, 6):
+            j = i - SKEWS[at]
+
+            @pl.when((j >= 0) & (j < nch))
+            def _():
+                steps[at](j)
+
+    @pl.loop(0, rows // 8)
+    def _(t):
+        block = y_acc[pl.ds(pl.multiple_of(t * 8, 8), 8), :]
+        for s in range(8 // own):
+            piece = jnp.concatenate(
+                [block[s * own : (s + 1) * own, c * w4 : (c + 1) * w4] for c in range(split)], axis=0
+            )
+            y_send[t * (8 // own) + s] = piece.astype(jnp.bfloat16)
+
+    def y_copy(to, source):
+        return pltpu.make_async_remote_copy(
+            src_ref=y_send.at[to],
+            dst_ref=y_recv.at[source],
+            send_sem=ys_sem.at[to],
+            recv_sem=yr_sem.at[source],
+            device_id=device(to),
+            device_id_type=MESH,
+        )
+
+    @pl.loop(1, n)
+    def _(k):
+        y_copy(lax.rem(me + k, n), me).start()
+
+    y_recv[me] = y_send[me]
+
+    @pl.loop(1, n)
+    def _(k):
+        other = lax.rem(me + k, n)
+        y_copy(other, other).wait_recv()
+
+    for f in range(FEAT_GROUPS):
+        branch = y_recv[f].astype(jnp.float32)
+        for q in range(1, n // FEAT_GROUPS):
+            branch += y_recv[q * FEAT_GROUPS + f].astype(jnp.float32)
+        for c in range(split):
+            at = f * width + c * w4
+            rows_in = leaf_ref[:, at : at + w4].astype(jnp.float32)
+            out_ref[:, at : at + w4] = (rows_in + branch[c * own : (c + 1) * own]).astype(jnp.bfloat16)
+
+    @pl.loop(1, n)
+    def _(k):
+        other = lax.rem(me + k, n)
+        x_copy(other, other).wait_send()
+        y_copy(other, other).wait_send()
+
+    @pl.loop(0, nch)
+    def _(j):
+        for stage in range(6):
+            copy_of(stage, j).wait_send()
+
+
+def fits(parts, count, own, width, hid_width, chunk):
+    n = parts * count
+    if own not in (2, 4, 8) or count % FEAT_GROUPS or hid_width % parts:
+        return False
+    half = hid_width // parts
+    rows = own * n
+    if half % chunk or rows % 128 or width % (16 // own * 128):
+        return False
+    need = half * width * 6 + half * rows * 12 + rows * width * 12
+    return need < VMEM_BYTES * 0.95
+
+
+def fused(parts, count, leaf_rows, norm_gain, gate_weight, up_weight, down_weight):
+    own, features = leaf_rows.shape
+    unused, width, hid_width = gate_weight.shape
+    half = hid_width // parts
+    chunk = CHUNK
+    nch = half // chunk
+    n = parts * count
+    rows = own * n
+    w4 = width // (16 // own)
+    bf16, f32 = jnp.bfloat16, jnp.float32
+    vmem = pl.BlockSpec(memory_space=pltpu.VMEM)
+    hbm = pl.BlockSpec(memory_space=pl.ANY)
+    dma = pltpu.SemaphoreType.DMA
+    return pl.pallas_call(
+        functools.partial(fused_kernel, (parts, count, own, width, half, chunk)),
+        out_shape=jax.ShapeDtypeStruct((own, features), bf16),
+        in_specs=[vmem, vmem, hbm, hbm, hbm],
+        out_specs=vmem,
+        scratch_shapes=[
+            pltpu.VMEM((nch, width, chunk), bf16),
+            pltpu.VMEM((nch, width, chunk), bf16),
+            pltpu.VMEM((nch, chunk, width), bf16),
+            pltpu.VMEM((FEAT_GROUPS, 16, w4), bf16),
+            pltpu.VMEM((n, 16, w4), bf16),
+            pltpu.VMEM((rows, width), bf16),
+            pltpu.VMEM((nch, rows // 2, 2 * chunk), f32),
+            pltpu.VMEM((nch, rows // 2, 2 * chunk), bf16),
+            pltpu.VMEM((nch, rows // 2, 2 * chunk), bf16),
+            pltpu.VMEM((nch, rows // 4, 2 * chunk), bf16),
+            pltpu.VMEM((nch, rows // 4, 2 * chunk), bf16),
+            pltpu.VMEM((nch, rows // 8, 2 * chunk), bf16),
+            pltpu.VMEM((nch, rows // 8, 2 * chunk), bf16),
+            pltpu.VMEM((nch, rows, chunk), bf16),
+            pltpu.VMEM((rows, width), f32),
+            pltpu.VMEM((n, 16, w4), bf16),
+            pltpu.VMEM((n, 16, w4), bf16),
+            dma((3, nch)),
+            dma((6, nch)),
+            dma((6, nch)),
+            dma((n,)),
+            dma((n,)),
+            dma((n,)),
+            dma((n,)),
+        ],
+        compiler_params=pltpu.CompilerParams(
+            collective_id=0, has_side_effects=True, vmem_limit_bytes=VMEM_BYTES
+        ),
+    )(leaf_rows, norm_gain.reshape(1, features), gate_weight, up_weight, down_weight)
 
 
 def swapped(value, axis, apart):
@@ -21,7 +347,7 @@
     return (values * inverse * norm_gain).astype(jnp.bfloat16)
 
 
-def per_device(leaf_rows, norm_gain, gate_weight, up_weight, down_weight):
+def plain(leaf_rows, norm_gain, gate_weight, up_weight, down_weight):
     gate_block = gate_weight[0]
     up_block = up_weight[0]
     down_block = down_weight[0]
@@ -82,6 +408,15 @@
 
 
 def solution(mesh):
+    parts, count = mesh.shape["parts"], mesh.shape["loop"]
+
+    def per_device(leaf_rows, norm_gain, gate_weight, up_weight, down_weight):
+        arrays = (leaf_rows, norm_gain, gate_weight, up_weight, down_weight)
+        unused, width, hid_width = gate_weight.shape
+        if fits(parts, count, leaf_rows.shape[0], width, hid_width, CHUNK):
+            return fused(parts, count, *arrays)
+        return plain(*arrays)
+
     return jax.shard_map(
         per_device,
         mesh=mesh,

time: 273 us -> 66.7 us (0.24)
  waiting for transfers between devices: 205 us -> 0 us
  Pallas kernels: 0 us -> 65 us
  matrix products: 33.9 us -> 0 us
  between operations: 13.7 us -> 0.01 us
  other arithmetic: 10.4 us -> 0 us
  starting transfers between devices: 4.69 us -> 0 us
  local copies, waits for them, and re-layouts: 4.98 us -> 1.49 us
    ppermute x10 -> x0, waiting for transfers between devices: 164 us -> none  [swapped(): return lax.ppermute(value, axis, pairs)]
    pallas_call x0 -> x1, Pallas kernels: none -> 65 us  [fused(): pl.pallas_call(functools.partial(fused_kernel, (parts, count, own, width,...]
    all_gather x1 -> x0, waiting for transfers between devices: 41 us -> none  [per_device(): lax.all_gather(normed, 'loop', axis=0, tiled=True)]
    dot_general x3 -> x0, matrix products: 33.9 us -> none  [the longest x1 11.3 us: per_device(): current = jnp.dot(hidden, down_block, preferred_element_type=jnp.float32)]
    ppermute x10 -> x0, starting transfers between devices: 4.69 us -> none  [swapped(): return lax.ppermute(value, axis, pairs)]
    add x4 -> x0, other arithmetic: 4.54 us -> none  [per_device(): current = keep + swapped(other, 'loop', bit)]
    unnamed x8 -> x1, local copies, waits for them, and re-layouts: 4.61 us -> 1.49 us
  transfers between devices with their start and end apart: 11 -> 0, of which waited for: 11 -> 0; matrix products, arithmetic and copies ran while one was open for 0% -> 0% of each run, Pallas kernels for 0% -> 0%
where the time goes in v1:
time: 66.7 us; the launch traced here: 66.5 us
  Pallas kernels  65 us (97%)
  local copies, waits for them, and re-layouts  1.49 us (2%)
    pallas_call x1, Pallas kernels, fused(): pl.pallas_call(functools.partial(fused_kernel, (parts, count, own, width,...  65 us
    unnamed x1, local copies, waits for them, and re-layouts  1.49 us

profile of v1, /device:TPU:0, one launch (start us, length us, event | category | flops | bytes accessed | tf_op | source)
XLA Modules:
  0.0 66.5 jit_solution(4567285650405996140)
XLA Ops:
  0.0 65.0 %shard_map.55 = bf16[4,8192]{1,0:T(4,128)(2,1)} custom-call(bf16[4,8192]{1,0:T(4,128)(2,1)} %leaf_ref.1, f32[1,8192]{1,0:T(1,128)} %bitcast.1, bf16[1,1024,13312]{2,1,0:T(8,128)(2,1)} %gate_hbm.1, bf16[1,1024,13312]{2,1,0:T(8,128)(2,1)} %up_hbm.1, bf16[1,13312,1024]{2,1,0:T(8,128)(2,1)} %down_hbm.1), custom_call_target="tpu_custom_call" | custom-call | tf_op jit(solution)/shard_map/pallas_call | solution.py:301
  65.0 1.5 %copy.7 = bf16[4,8192]{1,0:T(4,128)(2,1)} copy(bf16[4,8192]{1,0:T(4,128)(2,1)} %shard_map.55) | data formatting | bytes 131072

commit v2 on v1

--- a/solution.py
+++ b/solution.py
@@ -9,7 +9,7 @@
 
 FEAT_GROUPS = 8
 CHUNK = 512
-SKEWS = (0, 1, 3, 5, 7, 9, 10)
+SKEWS = (0, 4, 9, 14, 19, 24, 26)
 VMEM_BYTES = 60 * 2**20
 MESH = pl.DeviceIdType.MESH
 
@@ -20,7 +20,8 @@
     sizes, leaf_ref, gain_ref, gate_hbm, up_hbm, down_hbm, out_ref,
     gate_v, up_v, down_v, x_send, x_recv, x_full, keep,
     s1, r1, s2, r2, s3, r3, hid, y_acc, y_send, y_recv,
-    w_sem, send_sem, recv_sem, xs_sem, xr_sem, ys_sem, yr_sem,
+    y_far,
+    w_sem, send_sem, recv_sem, xs_sem, xr_sem, ys_sem, yr_sem, block_sem,
 ):
     parts, count, own, width, half, chunk = sizes
     n = parts * count
@@ -40,6 +41,24 @@
     def device(index):
         return {"parts": index // count, "loop": lax.rem(index, count)}
 
+    feat = lax.rem(place, FEAT_GROUPS)
+    near_base = place - feat
+    far_base = FEAT_GROUPS - near_base
+    far_mine = part * count + far_base
+    far_other = (1 - part) * count + far_base
+
+    def near(k):
+        inner = lax.rem(part * FEAT_GROUPS + feat + k, 2 * FEAT_GROUPS)
+        return inner // FEAT_GROUPS * count + near_base + lax.rem(inner, FEAT_GROUPS)
+
+    def far(k):
+        return far_mine + lax.rem(feat + k, FEAT_GROUPS)
+
+    some = FEAT_GROUPS // 2
+
+    def across(k):
+        return far_other + lax.rem(feat + k, FEAT_GROUPS)
+
     def bits(j):
         even = 1 - lax.rem(j, 2)
         odd = 1 - even
@@ -71,11 +90,12 @@
 
     barrier = pltpu.get_barrier_semaphore()
 
+    def greet(other):
+        pl.semaphore_signal(barrier, inc=1, device_id=device(other), device_id_type=MESH)
+
     @pl.loop(1, n)
     def _(k):
-        pl.semaphore_signal(
-            barrier, inc=1, device_id=device(lax.rem(me + k, n)), device_id_type=MESH
-        )
+        greet(lax.rem(me + k, n))
 
     values = leaf_ref[...].astype(jnp.float32)
     inverse = lax.rsqrt(jnp.mean(values * values, axis=1, keepdims=True) + epsilon)
@@ -86,6 +106,7 @@
         )
         x_send[f] = piece.astype(jnp.bfloat16)
     y_acc[...] = jnp.zeros_like(y_acc)
+    y_recv[...] = jnp.zeros_like(y_recv)
     x_recv[me] = x_send[lax.rem(place, FEAT_GROUPS)]
 
     pl.semaphore_wait(barrier, n - 1)
@@ -100,14 +121,47 @@
             device_id_type=MESH,
         )
 
-    @pl.loop(1, n)
-    def _(k):
-        x_copy(lax.rem(me + k, n), me).start()
-
-    @pl.loop(1, n)
-    def _(k):
-        other = lax.rem(me + k, n)
-        x_copy(other, other).wait_recv()
+    def x_forward(base):
+        block = x_recv.at[pl.ds(base, some)]
+        return pltpu.make_async_remote_copy(
+            src_ref=block,
+            dst_ref=block,
+            send_sem=block_sem.at[0],
+            recv_sem=block_sem.at[1],
+            device_id={"parts": 1 - part, "loop": place},
+            device_id_type=MESH,
+        )
+
+    @pl.loop(0, FEAT_GROUPS)
+    def _(k):
+        x_copy(far(k), me).start()
+
+    @pl.when(feat >= some)
+    def _():
+        @pl.loop(0, FEAT_GROUPS)
+        def _(k):
+            x_copy(across(k), me).start()
+
+    @pl.loop(1, 2 * FEAT_GROUPS)
+    def _(k):
+        x_copy(near(k), me).start()
+
+    @pl.loop(0, some)
+    def _(k):
+        x_copy(far_mine + k, far_mine + k).wait_recv()
+
+    x_forward(far_mine).start()
+
+    @pl.loop(some, FEAT_GROUPS)
+    def _(k):
+        x_copy(far_mine + k, far_mine + k).wait_recv()
+        x_copy(far_other + k, far_other + k).wait_recv()
+
+    @pl.loop(1, 2 * FEAT_GROUPS)
+    def _(k):
+        x_copy(near(k), near(k)).wait_recv()
+
+    x_forward(far_other).wait_recv()
 
     group = 16 // own
     for t in range(rows // 16):
@@ -231,6 +285,16 @@
             )
             y_send[t * (8 // own) + s] = piece.astype(jnp.bfloat16)
 
+    y_block = pltpu.make_async_remote_copy(
+        src_ref=y_send.at[pl.ds(far_other, some)],
+        dst_ref=y_far,
+        send_sem=block_sem.at[2],
+        recv_sem=block_sem.at[3],
+        device_id={"parts": 1 - part, "loop": place},
+        device_id_type=MESH,
+    )
+    y_block.start()
+
     def y_copy(to, source):
         return pltpu.make_async_remote_copy(
             src_ref=y_send.at[to],
@@ -241,41 +305,84 @@
             device_id_type=MESH,
         )
 
-    @pl.loop(1, n)
-    def _(k):
-        y_copy(lax.rem(me + k, n), me).start()
+    @pl.loop(some, FEAT_GROUPS)
+    def _(k):
+        y_copy(far_mine + k, me).start()
+        y_copy(far_other + k, me).start()
+
+    @pl.loop(1, 2 * FEAT_GROUPS)
+    def _(k):
+        y_copy(near(k), me).start()
 
     y_recv[me] = y_send[me]
-
-    @pl.loop(1, n)
-    def _(k):
-        other = lax.rem(me + k, n)
-        y_copy(other, other).wait_recv()
+    mine = pl.ds(far_mine, some)
+    y_block.wait_recv()
+    both_parts = y_send[mine].astype(jnp.float32) + y_far[...].astype(jnp.float32)
+    y_send[mine] = both_parts.astype(jnp.bfloat16)
+
+    @pl.loop(0, some)
+    def _(k):
+        y_copy(far_mine + k, me).start()
+
+    x_forward(far_mine).wait_send()
+    y_block.wait_send()
+
+    @pl.loop(0, FEAT_GROUPS)
+    def _(k):
+        x_copy(far(k), far(k)).wait_send()
+
+    @pl.when(feat >= some)
+    def _():
+        @pl.loop(0, FEAT_GROUPS)
+        def _(k):
+            x_copy(across(k), across(k)).wait_send()
+
+    @pl.loop(1, 2 * FEAT_GROUPS)
+    def _(k):
+        x_copy(near(k), near(k)).wait_send()
+        y_copy(near(k), near(k)).wait_send()
+
+    @pl.loop(0, nch)
+    def _(j):
+        for stage in range(6):
+            copy_of(stage, j).wait_send()
+
+    @pl.loop(1, 2 * FEAT_GROUPS)
+    def _(k):
+        y_copy(near(k), near(k)).wait_recv()
+
+    @pl.loop(0, FEAT_GROUPS)
+    def _(k):
+        y_copy(far(k), far(k)).wait_recv()
+
+    @pl.when(feat >= some)
+    def _():
+        @pl.loop(0, FEAT_GROUPS)
+        def _(k):
+            y_copy(across(k), across(k)).wait_recv()
 
     for f in range(FEAT_GROUPS):
-        branch = y_recv[f].astype(jnp.float32)
-        for q in range(1, n // FEAT_GROUPS):
-            branch += y_recv[q * FEAT_GROUPS + f].astype(jnp.float32)
+        branch = y_recv[part * count + near_base + f].astype(jnp.float32)
+        branch += y_recv[(1 - part) * count + near_base + f].astype(jnp.float32)
+        branch += y_recv[far_mine + f].astype(jnp.float32)
+        branch += y_recv[far_other + f].astype(jnp.float32)
         for c in range(split):
             at = f * width + c * w4
             rows_in = leaf_ref[:, at : at + w4].astype(jnp.float32)
             out_ref[:, at : at + w4] = (rows_in + branch[c * own : (c + 1) * own]).astype(jnp.bfloat16)
 
-    @pl.loop(1, n)
-    def _(k):
-        other = lax.rem(me + k, n)
-        x_copy(other, other).wait_send()
-        y_copy(other, other).wait_send()
-
-    @pl.loop(0, nch)
-    def _(j):
-        for stage in range(6):
-            copy_of(stage, j).wait_send()
+    @pl.loop(0, FEAT_GROUPS)
+    def _(k):
+        y_copy(far(k), far(k)).wait_send()
+
+    @pl.loop(some, FEAT_GROUPS)
+    def _(k):
+        y_copy(far_other + k, far_other + k).wait_send()
 
 
 def fits(parts, count, own, width, hid_width, chunk):
     n = parts * count
-    if own not in (2, 4, 8) or count % FEAT_GROUPS or hid_width % parts:
+    if own not in (2, 4, 8) or count != 2 * FEAT_GROUPS or parts != 2 or hid_width % parts:
         return False
     half = hid_width // parts
     rows = own * n
@@ -321,6 +428,7 @@
             pltpu.VMEM((rows, width), f32),
             pltpu.VMEM((n, 16, w4), bf16),
             pltpu.VMEM((n, 16, w4), bf16),
+            pltpu.VMEM((FEAT_GROUPS // 2, 16, w4), bf16),
             dma((3, nch)),
             dma((6, nch)),
             dma((6, nch)),
@@ -328,6 +436,7 @@
             dma((n,)),
             dma((n,)),
             dma((n,)),
+            dma((4,)),
         ],
         compiler_params=pltpu.CompilerParams(
             collective_id=0, has_side_effects=True, vmem_limit_bytes=VMEM_BYTES

time: 66.7 us -> 57.1 us (0.86)
  Pallas kernels: 65 us -> 55.4 us
    pallas_call x1, Pallas kernels: 65 us -> 55.4 us  [fused(): pl.pallas_call(functools.partial(fused_kernel, (parts, count, own, width,...]
where the time goes in v2:
time: 57.1 us; the launch traced here: 56.9 us
  Pallas kernels  55.4 us (97%)
  local copies, waits for them, and re-layouts  1.49 us (3%)
    pallas_call x1, Pallas kernels, fused(): pl.pallas_call(functools.partial(fused_kernel, (parts, count, own, width,...  55.4 us
    unnamed x1, local copies, waits for them, and re-layouts  1.49 us

profile of v2, /device:TPU:0, one launch (start us, length us, event | category | flops | bytes accessed | tf_op | source)
XLA Modules:
  0.0 56.9 jit_solution(15979529824482327954)
XLA Ops:
  0.0 55.4 %shard_map.55 = bf16[4,8192]{1,0:T(4,128)(2,1)} custom-call(bf16[4,8192]{1,0:T(4,128)(2,1)} %leaf_ref.1, f32[1,8192]{1,0:T(1,128)} %bitcast.1, bf16[1,1024,13312]{2,1,0:T(8,128)(2,1)} %gate_hbm.1, bf16[1,1024,13312]{2,1,0:T(8,128)(2,1)} %up_hbm.1, bf16[1,13312,1024]{2,1,0:T(8,128)(2,1)} %down_hbm.1), custom_call_target="tpu_custom_call" | custom-call | tf_op jit(solution)/shard_map/pallas_call | solution.py:408
  55.4 1.5 %copy.7 = bf16[4,8192]{1,0:T(4,128)(2,1)} copy(bf16[4,8192]{1,0:T(4,128)(2,1)} %shard_map.55) | data formatting | bytes 131072

commit v3 on v2

--- a/solution.py
+++ b/solution.py
@@ -9,7 +9,7 @@
 
 FEAT_GROUPS = 8
 CHUNK = 512
-SKEWS = (0, 4, 9, 14, 19, 24, 26)
+SKEWS = (0, 4, 10, 17, 24, 31, 33)
 VMEM_BYTES = 60 * 2**20
 MESH = pl.DeviceIdType.MESH
 

time: 57.1 us -> 56 us (0.981)
  Pallas kernels: 55.4 us -> 54.3 us
    pallas_call x1, Pallas kernels: 55.4 us -> 54.3 us  [fused(): pl.pallas_call(functools.partial(fused_kernel, (parts, count, own, width,...]
where the time goes in v3:
time: 56 us; the launch traced here: 55.8 us
  Pallas kernels  54.3 us (97%)
  local copies, waits for them, and re-layouts  1.49 us (3%)
    pallas_call x1, Pallas kernels, fused(): pl.pallas_call(functools.partial(fused_kernel, (parts, count, own, width,...  54.3 us
    unnamed x1, local copies, waits for them, and re-layouts  1.49 us

profile of v3, /device:TPU:0, one launch (start us, length us, event | category | flops | bytes accessed | tf_op | source)
XLA Modules:
  0.0 55.8 jit_solution(13931979996064461506)
XLA Ops:
  0.0 54.3 %shard_map.55 = bf16[4,8192]{1,0:T(4,128)(2,1)} custom-call(bf16[4,8192]{1,0:T(4,128)(2,1)} %leaf_ref.1, f32[1,8192]{1,0:T(1,128)} %bitcast.1, bf16[1,1024,13312]{2,1,0:T(8,128)(2,1)} %gate_hbm.1, bf16[1,1024,13312]{2,1,0:T(8,128)(2,1)} %up_hbm.1, bf16[1,13312,1024]{2,1,0:T(8,128)(2,1)} %down_hbm.1), custom_call_target="tpu_custom_call" | custom-call | tf_op jit(solution)/shard_map/pallas_call | solution.py:408
  54.3 1.5 %copy.7 = bf16[4,8192]{1,0:T(4,128)(2,1)} copy(bf16[4,8192]{1,0:T(4,128)(2,1)} %shard_map.55) | data formatting | bytes 131072
